TPU v7x, 32 devices: a whole 2x2x4 slice. The times are simulated.
32 devices in a mesh: row: 8 (over z, x), col: 4 (over y, core).
Axes of the slice: x: 2, y: 2, z: 4, core: 2. Of those that a mesh axis runs over, the one named last changes fastest.
Arguments:
- psi: bfloat16 [1024, 16, 512], P('row', None, 'col'), may hold values from -6 to 6
- env_left: bfloat16 [8, 3, 128, 128, 34], P('row'), may hold values from -0.0546875 to 0.0546875
- env_right: bfloat16 [4, 3, 128, 34, 128], P('col'), may hold values from -0.3125 to 0.3125
- first_site_operator: bfloat16 [34, 34, 4, 4], replicated, may hold values from -0.5 to 0.5
- mpo_right: bfloat16 [34, 34, 4, 4], replicated, may hold values from -0.5 to 0.5
- block_mask: int32 [8, 4], P('row', 'col'), may hold values 0 or 1
- left_live: int32 [8], P('row'), may hold values from 64 to 128, as said below
- right_live: int32 [4], P('col'), may hold values from 64 to 128, as said below
Outputs:
- hpsi: bfloat16 [1024, 16, 512], P('row', None, 'col')
- residual: bfloat16 [1024, 16, 512], P('row', None, 'col')
- quotient: float32 [], replicated
Inputs may be any that keep to these rules, and one draw needn't show every extreme that they name: `left_live`: a block is either full or is the last block of a sector with fewer live states; some block is full. `right_live`: a block is either full or is the last block of a sector with fewer live states; some block is full.
All inputs are finite; a program needn't handle non-finite values. No bound on the sum of `block_mask` on one device may be relied on, other than what follows from the above.
Results may differ from a plain program's by a relative error of at most 0.0064.
Values may be sent and summed in bfloat16 or wider, within the bound.
A program may use at most 192 MiB of HBM per device.

v0:
```python
import jax
import jax.numpy as jnp
from jax import lax
from jax.sharding import PartitionSpec as P


def padded(block, sides, width):
    for axis, dim in sides:
        count = lax.axis_size(axis)
        forward = [(i, i + 1) for i in range(count - 1)]
        backward = [(target, source) for source, target in forward]
        low = lax.ppermute(
            lax.slice_in_dim(block, block.shape[dim] - width, None, axis=dim), axis, forward
        )
        high = lax.ppermute(lax.slice_in_dim(block, 0, width, axis=dim), axis, backward)
        block = jnp.concatenate([low, block, high], axis=dim)
    return block


def from_behind(block, axis, distance):
    devices = range(lax.axis_size(axis))
    route = [(i - distance, i) for i in devices if i - distance in devices]
    return lax.ppermute(block, axis, route)


def live_pattern(block_mask, left_live, right_live, block_rows):
    inside = lax.broadcasted_iota(jnp.int32, (block_rows,), 0)
    row_ok = (inside[None, :] < left_live[:, None]).reshape(-1)
    col_ok = (inside[None, :] < right_live[:, None]).reshape(-1)
    expanded = jnp.repeat(jnp.repeat(block_mask, block_rows, axis=0), block_rows, axis=1)
    return (expanded > 0) & row_ok[:, None] & col_ok[None, :]


def on_device(
    psi, env_left, env_right, first_site_operator, mpo_right, block_mask, left_live, right_live
):
    blocks = env_left.shape[0]
    block_rows = env_left.shape[2]
    mpo_width = env_left.shape[4]
    states = psi.shape[1]
    site_states = first_site_operator.shape[2]
    live_mask = live_pattern(block_mask, left_live, right_live, block_rows)
    masked_wavefunction = psi * live_mask[:, None, :].astype(jnp.bfloat16)
    widened = padded(masked_wavefunction, (("col", 2),), block_rows)
    right_matrix = env_right[0].reshape(3 * block_rows, mpo_width * block_rows)
    strip = widened.reshape(block_rows * states, 3 * block_rows)
    section_one = jnp.dot(strip, right_matrix, preferred_element_type=jnp.float32).astype(
        jnp.bfloat16
    )
    section_one = section_one.reshape(block_rows, site_states, site_states, mpo_width, block_rows)
    second_section = jnp.einsum(
        "mnts,xasnb->xamtb", mpo_right, section_one, preferred_element_type=jnp.float32
    ).astype(jnp.bfloat16)
    third_section = jnp.einsum(
        "dquo,woqzj->wduzj", first_site_operator, second_section, preferred_element_type=jnp.float32
    ).astype(jnp.bfloat16)
    outcomes = [third_section.reshape(block_rows * mpo_width, states * block_rows)]

    def couple_left(coupling, operand):
        return jnp.dot(
            coupling.reshape(block_rows, block_rows * mpo_width),
            operand,
            preferred_element_type=jnp.float32,
        )

    running = couple_left(env_left[0, 1], outcomes[0])
    totals = [running]
    from_prev = from_behind(outcomes[blocks - 1], "row", 1)
    from_next = from_behind(outcomes[0], "row", -1)
    totals[0] = totals[0] + couple_left(env_left[0, 0], from_prev)
    totals[blocks - 1] = totals[blocks - 1] + couple_left(env_left[blocks - 1, 2], from_next)
    hamiltonian_times_wavefunction = jnp.stack(totals).reshape(
        blocks * block_rows, states, block_rows
    )
    live_float = live_mask[:, None, :].astype(jnp.float32)
    applied = hamiltonian_times_wavefunction * live_float
    psi_float = masked_wavefunction.astype(jnp.float32)
    numerator, denominator = lax.psum(
        (jnp.sum(psi_float * applied), jnp.sum(psi_float * psi_float)), ("row", "col")
    )
    quotient = numerator / (denominator + 1e-06)
    return (
        applied.astype(jnp.bfloat16),
        (applied - quotient * psi_float).astype(jnp.bfloat16),
        quotient,
    )


def solution(mesh):
    return jax.shard_map(
        on_device,
        mesh=mesh,
        in_specs=(
            P("row", None, "col"),
            P("row", None, None, None, None),
            P("col", None, None, None, None),
            P(),
            P(),
            P("row", "col"),
            P("row"),
            P("col"),
        ),
        out_specs=(P("row", None, "col"), P("row", None, "col"), P()),
        check_vma=False,
    )
```

profile of v0, /device:TPU:0, one launch (start us, length us, event | category | flops | bytes accessed | tf_op | source)
XLA Modules:
  0.0 980.7 jit_solution(9273195986214550080)
XLA Ops:
  3.8 2.4 collective-permute-start
  6.2 1.3 collective-permute-start.1
  7.5 4.2 copy.13
  12.4 12.6 %convolution_convert_fusion = bf16[2048,4352]{1,0:T(8,128)(2,1)} fusion(bf16[2048,384]{1,0:T(8,128)(2,1)S(1)} %bitcast.74, bf16[48,8,34,128]{3,2,1,0:T(8,128)(2,1)S(1)} %bitcast.73), kind=kOutput, calls=%fused_computation.7 | convolution fusion | flops 6854017024 | bytes 22740992 | tf_op jit(solution)/shard_map/dot_general | solution.py:47
  24.9 29.7 %reshape.85 = bf16[128,4,4,34,128,1]{4,3,2,1,0,5:T(8,128)(2,1)} reshape(bf16[2048,4352]{1,0:T(8,128)(2,1)} %convolution_convert_fusion) | data formatting | bytes 35651584 | tf_op jit(solution)/shard_map/reshape | solution.py:50
  54.6 21.4 %fusion.39 = bf16[128,4,34,4,128,1]{4,2,1,5,3,0:T(8,128)(2,1)} fusion(bf16[128,4,4,34,128,1]{4,3,2,1,0,5:T(8,128)(2,1)} %reshape.85, bf16[34,34,4,4,1,1]{1,3,2,0,4,5:T(4,128)(2,1)S(1)} %bitcast.72), kind=kOutput, calls=%fused_computation.2.clone.clone.clone.clone.1 | convolution fusion | flops 2433220608 | bytes 35688576 | tf_op jit(solution)/shard_map/mnts,xasnb->xamtb/dot_general | solution.py:51
  76.0 21.3 %fusion.3 = bf16[128,34,4,4,128]{4,1,2,3,0:T(8,128)(2,1)} fusion(bf16[34,34,4,4,1,1]{1,3,2,0,5,4:T(4,128)(2,1)S(1)} %bitcast.76, bf16[128,4,34,4,128,1]{4,2,1,5,3,0:T(8,128)(2,1)} %fusion.39), kind=kOutput, calls=%fused_computation.4 | convolution fusion | flops 2433220608 | bytes 35688576 | tf_op jit(solution)/shard_map/dquo,woqzj->wduzj/dot_general | solution.py:54
  97.3 17.6 %copy.15 = bf16[128,34,4,4,128]{4,3,2,1,0:T(4,128)(2,1)} copy(bf16[128,34,4,4,128]{4,1,2,3,0:T(8,128)(2,1)} %fusion.3) | data formatting | bytes 35651584 | tf_op jit(solution)/shard_map/convert_element_type | solution.py:56
  114.9 29.3 %reshape.84 = bf16[4352,2048]{1,0:T(8,128)(2,1)} reshape(bf16[128,34,4,4,128]{4,3,2,1,0:T(4,128)(2,1)} %copy.15) | data formatting | bytes 35651584 | tf_op jit(solution)/shard_map/reshape | solution.py:57
  144.3 10.0 %collective-permute-start.2 = (bf16[4352,2048]{1,0:T(8,128)(2,1)}, bf16[4352,2048]{1,0:T(8,128)(2,1)}, u32[]{:S(2)}, u32[]{:S(2)}) collective-permute-start(bf16[4352,2048]{1,0:T(8,128)(2,1)} %reshape.84), channel_id=1, source_target_pairs={{0,4},{4,8},{8,12},{12,16},{16,20},{20,24},{24,28},{1,5},{5,9},{9,... | collective-permute-start | bytes 53477384 | tf_op jit(solution)/shard_map/ppermute | solution.py:23
  154.2 1.3 collective-permute-start.3
  155.5 3.7 fusion.21
  159.2 2.1 copy.16
  161.3 1.2 reshape_squeeze.13
  162.5 2.1 copy.17
  164.7 1.2 reshape_squeeze.14
  165.9 1.4 copy.18
  167.7 9.0 fusion.22
  176.7 732.2 %collective-permute-done.2 = bf16[4352,2048]{1,0:T(8,128)(2,1)} collective-permute-done((bf16[4352,2048]{1,0:T(8,128)(2,1)}, bf16[4352,2048]{1,0:T(8,128)(2,1)}, u32[]{:S(2)}, u32[]{:S(2)}) %collective-permute-start.2) | collective-permute-done | bytes 17825824 | tf_op jit(solution)/shard_map/ppermute | solution.py:23
  908.9 8.9 convolution_add_fusion.1
  917.8 9.9 %convolution_add_fusion = f32[2048,128]{1,0:T(8,128)} fusion(f32[2048,128]{1,0:T(8,128)S(1)} %convolution_add_fusion.1, bf16[4352,2048]{1,0:T(8,128)(2,1)} %collective-permute-done.3, bf16[128,4352]{0,1:T(8,128)(2,1)S(1)} %reshape_squeeze.15), kind=kOutput, calls=%fused_computation.10 | convolution fusion | flops 2281963520 | bytes 21037056 | tf_op jit(solution)/shard_map/dot_general | solution.py:60
  927.7 1.7 copy.19
  930.4 46.6 %all-reduce = (f32[]{:T(128)}, f32[]{:T(128)}) all-reduce(f32[]{:T(128)} %get-tuple-element.4, f32[]{:T(128)} %get-tuple-element.3), channel_id=1, replica_groups=mesh['row'=8,'col'=4] {'row','col'}, use_global_device_ids=true, to_apply=%region_1.0 | all-reduce | flops 2 | bytes 16 | tf_op jit(solution)/shard_map/psum | solution.py:78
  978.3 1.3 fusion.17
  (19 shorter events, 3.2 us)
Async XLA Ops:
  0.6 54.0 %copy-start = (bf16[34,34,4,4]{1,3,2,0:T(4,128)(2,1)S(1)}, bf16[34,34,4,4]{1,3,2,0:T(4,128)(2,1)}, u32[]{:S(2)}) copy-start(bf16[34,34,4,4]{1,3,2,0:T(4,128)(2,1)} %param.12) | copy-start | bytes 110980
  3.8 7.9 collective-permute-start
  6.2 5.9 collective-permute-start.1
  54.6 21.4 %copy-start.4 = (bf16[34,34,4,4]{1,3,2,0:T(4,128)(2,1)S(1)}, bf16[34,34,4,4]{1,3,2,0:T(4,128)(2,1)}, u32[]{:S(2)}) copy-start(bf16[34,34,4,4]{1,3,2,0:T(4,128)(2,1)} %param.11) | copy-start | bytes 110980
  144.3 764.7 %collective-permute-start.2 = (bf16[4352,2048]{1,0:T(8,128)(2,1)}, bf16[4352,2048]{1,0:T(8,128)(2,1)}, u32[]{:S(2)}, u32[]{:S(2)}) collective-permute-start(bf16[4352,2048]{1,0:T(8,128)(2,1)} %reshape.84), channel_id=1, source_target_pairs={{0,4},{4,8},{8,12},{12,16},{16,20},{20,24},{24,28},{1,5},{5,9},{9,... | collective-permute-start | bytes 53477384 | tf_op jit(solution)/shard_map/ppermute | solution.py:23
  154.2 763.6 %collective-permute-start.3 = (bf16[4352,2048]{1,0:T(8,128)(2,1)}, bf16[4352,2048]{1,0:T(8,128)(2,1)}, u32[]{:S(2)}, u32[]{:S(2)}) collective-permute-start(bf16[4352,2048]{1,0:T(8,128)(2,1)} %reshape.84), channel_id=1, source_target_pairs={{4,0},{8,4},{12,8},{16,12},{20,16},{24,20},{28,24},{5,1},{9,5},{13... | collective-permute-start | bytes 53477384 | tf_op jit(solution)/shard_map/ppermute | solution.py:23
  167.7 741.2 %copy-start.3 = (bf16[128,4352]{0,1:T(8,128)(2,1)S(1)}, bf16[128,4352]{0,1:T(8,128)(2,1)}, u32[]{:S(2)}) copy-start(bf16[128,4352]{0,1:T(8,128)(2,1)} %reshape_squeeze.14) | copy-start | bytes 3342340
  917.8 11.6 %copy-start.2 = (bf16[128,16,128]{2,1,0:T(8,128)(2,1)S(1)}, bf16[128,16,128]{2,1,0:T(8,128)(2,1)}, u32[]{:S(2)}) copy-start(bf16[128,16,128]{2,1,0:T(8,128)(2,1)} %param.8) | copy-start | bytes 1572868
  917.8 61.7 %copy-start.1 = (bf16[34,34,4,4]{1,3,2,0:T(4,128)(2,1)S(1)}, bf16[34,34,4,4]{1,3,2,0:T(4,128)(2,1)}, u32[]{:S(2)}) copy-start(bf16[34,34,4,4]{1,3,2,0:T(4,128)(2,1)} %param.12) | copy-start | bytes 110980
where the time goes:
time: 983 us; the launch traced here: 981 us
  waiting for transfers between devices  733 us (75%)
  local copies, waits for them, and re-layouts  94.7 us (10%)
  matrix products  82.9 us (8%)
  blocking collectives  46.6 us (5%)
  starting transfers between devices  14.9 us (2%)
    ppermute x2, waiting for transfers between devices, from_behind(): return lax.ppermute(block, axis, route)  732 us
    psum x1, blocking collectives, on_device(): lax.psum((jnp.sum(psi_float * applied), jnp.sum(psi_float * psi_float)),...  46.6 us
    reshape x1, local copies, waits for them, and re-layouts, on_device(): section_one.reshape(block_rows, site_states, site_states, mpo_width, bloc...  29.7 us
    reshape x1, local copies, waits for them, and re-layouts, on_device(): third_section.reshape(block_rows * mpo_width, states * block_rows)  29.3 us
    dot_general x3, matrix products, couple_left(): jnp.dot(coupling.reshape(block_rows, block_rows * mpo_width), operand, pr...  27.7 us
    dot_general x1, matrix products, on_device(): jnp.einsum('mnts,xasnb->xamtb', mpo_right, section_one, preferred_element...  21.4 us
    dot_general x1, matrix products, on_device(): jnp.einsum('dquo,woqzj->wduzj', first_site_operator, second_section, pref...  21.3 us
  transfers between devices with their start and end apart: 4, of which 2 were waited for; matrix products, arithmetic and copies ran while one was open for 3% of the time, Pallas kernels for 0%

commit v1 on v0

v1 whole, which is shorter than its diff:
```python
import functools

import jax
import jax.numpy as jnp
from jax import lax
from jax.experimental import pallas as pl
from jax.experimental.pallas import tpu as pltpu
from jax.sharding import PartitionSpec as P

CHUNK = 16
N_PAD = 40
M_PAD = 48


def from_behind(block, axis, distance):
    devices = range(lax.axis_size(axis))
    route = [(i - distance, i) for i in devices if i - distance in devices]
    return lax.ppermute(block, axis, route)


def shared_from_behind(coupling, distance):
    share = coupling.shape[0] // lax.axis_size("col")
    own = lax.dynamic_slice_in_dim(coupling, lax.axis_index("col") * share, share, 0)
    moved = from_behind(own, "row", distance)
    return lax.all_gather(moved, "col", axis=0, tiled=True)


def right_kernel(psi_ref, env_ref, site_ref, two_ref, one):
    rows = psi_ref.shape[0]
    depth, width, inside, lanes = env_ref.shape
    sites = site_ref.shape[1] // N_PAD

    @pl.when(pl.program_id(0) == 0)
    def _():
        one[...] = jnp.zeros_like(one)

    for w in range(0, width, 2):
        env = jnp.concatenate(
            [
                jnp.concatenate([env_ref[k, w + j] for k in range(depth)], axis=0)
                for j in range(2)
            ],
            axis=1,
        )
        found = jnp.dot(psi_ref[...], env, preferred_element_type=jnp.float32)
        for j in range(2):
            one[pl.ds(w + j, rows, stride=N_PAD), :] = found[:, j * lanes : (j + 1) * lanes]

    tall = sites * N_PAD

    def pair(i, _):
        start = pl.multiple_of(i * (2 * tall), 2 * tall)
        operand = jnp.concatenate(
            [one[pl.ds(start + j * tall, tall), :].astype(jnp.bfloat16) for j in range(2)], axis=1
        )
        found = jnp.dot(
            site_ref[...], operand, preferred_element_type=jnp.float32
        ).astype(jnp.bfloat16)
        for t in range(sites):
            for j in range(2):
                spot = pl.multiple_of((i * 2 + j) * M_PAD, M_PAD)
                two_ref[t, pl.ds(spot, M_PAD), :] = found[
                    t * M_PAD : (t + 1) * M_PAD, j * lanes : (j + 1) * lanes
                ]
        return 0

    lax.fori_loop(0, rows // sites // 2, pair, 0, unroll=8)


def right_part(widened, env, site):
    rows, depth = widened.shape
    lanes = env.shape[3]
    sites = site.shape[0] // M_PAD
    states = sites * sites
    block = CHUNK * states
    tall = rows // sites * M_PAD
    return pl.pallas_call(
        right_kernel,
        grid=(rows // block,),
        in_specs=[
            pl.BlockSpec((block, depth), lambda i: (i, 0)),
            pl.BlockSpec(env.shape, lambda i: (0, 0, 0, 0)),
            pl.BlockSpec(site.shape, lambda i: (0, 0)),
        ],
        out_specs=pl.BlockSpec((sites, CHUNK * sites * M_PAD, lanes), lambda i: (0, i, 0)),
        out_shape=jax.ShapeDtypeStruct((sites, tall, lanes), jnp.bfloat16),
        scratch_shapes=[pltpu.VMEM((block * N_PAD, lanes), jnp.float32)],
        compiler_params=pltpu.CompilerParams(vmem_limit_bytes=48 * 2**20),
        cost_estimate=pl.CostEstimate(
            flops=2 * rows * depth * env.shape[1] * lanes * 2,
            bytes_accessed=2 * sites * tall * lanes,
            transcendentals=0,
        ),
        name="right_part",
    )(widened, env, site)


def left_kernel(two_ref, site_ref, env_ref, psi_ref, own_ref, sent_ref, dot_ref, three, total):
    step = pl.program_id(0)
    lanes = two_ref.shape[2]
    sites = site_ref.shape[0] // M_PAD
    tall = sites * M_PAD
    block_rows = own_ref.shape[0]

    for x in range(0, CHUNK, 2):
        operand = jnp.concatenate(
            [two_ref[0, (x + j) * tall : (x + j + 1) * tall, :] for j in range(2)], axis=1
        )
        found = jnp.dot(
            site_ref[...], operand, preferred_element_type=jnp.float32
        ).astype(jnp.bfloat16)
        for j in range(2):
            for r in range(sites):
                three[(x + j) * M_PAD : (x + j + 1) * M_PAD, r * lanes : (r + 1) * lanes] = found[
                    r * M_PAD : (r + 1) * M_PAD, j * lanes : (j + 1) * lanes
                ]
    part = jnp.dot(env_ref[...], three[...], preferred_element_type=jnp.float32)

    @pl.when(step == 0)
    def _():
        total[...] = part

    @pl.when(step > 0)
    def _():
        total[...] += part

    @pl.when(step == pl.num_programs(0) - 1)
    def _():
        whole = total[...]
        own_ref[...] = whole[:block_rows]
        sent_ref[...] = whole[block_rows:].astype(jnp.bfloat16)
        weighed = psi_ref[0].astype(jnp.float32) * whole
        dot_ref[...] = jnp.sum(weighed.reshape(-1, 8, weighed.shape[1]), axis=0)


def left_part(two, site, env, psi_rows, t):
    lanes = two.shape[2]
    sites = site.shape[0] // M_PAD
    steps = two.shape[1] // (CHUNK * sites * M_PAD)
    tall, wide = env.shape[0], sites * lanes
    block_rows = tall // 3
    return pl.pallas_call(
        left_kernel,
        grid=(steps,),
        in_specs=[
            pl.BlockSpec((1, CHUNK * sites * M_PAD, lanes), lambda i: (t, i, 0)),
            pl.BlockSpec(site.shape, lambda i: (0, 0)),
            pl.BlockSpec((tall, CHUNK * M_PAD), lambda i: (0, i)),
            pl.BlockSpec((1, tall, wide), lambda i: (t, 0, 0)),
        ],
        out_specs=[
            pl.BlockSpec((block_rows, wide), lambda i: (0, 0)),
            pl.BlockSpec((2 * block_rows, wide), lambda i: (0, 0)),
            pl.BlockSpec((8, wide), lambda i: (0, 0)),
        ],
        out_shape=[
            jax.ShapeDtypeStruct((block_rows, wide), jnp.float32),
            jax.ShapeDtypeStruct((2 * block_rows, wide), jnp.bfloat16),
            jax.ShapeDtypeStruct((8, wide), jnp.float32),
        ],
        scratch_shapes=[
            pltpu.VMEM((CHUNK * M_PAD, wide), jnp.bfloat16),
            pltpu.VMEM((tall, wide), jnp.float32),
        ],
        compiler_params=pltpu.CompilerParams(vmem_limit_bytes=40 * 2**20),
        cost_estimate=pl.CostEstimate(
            flops=2 * tall * env.shape[1] * wide * 2,
            bytes_accessed=2 * two.shape[1] * lanes + 2 * tall * env.shape[1],
            transcendentals=0,
        ),
        name="left_part",
    )(two, site, env, psi_rows)


def sum_kernel(sizes, value_ref, out_ref, col_slots, row_slots, sems, recv_sems):
    rows, cols = sizes
    row, col = lax.axis_index("row"), lax.axis_index("col")
    peers = [((row, lax.rem(col + d, cols)), col_slots, d) for d in range(1, cols)]
    others = [((lax.rem(row + d, rows), col), row_slots, d) for d in range(1, rows)]
    barrier = pltpu.get_barrier_semaphore()
    for place, _, _ in peers + others:
        pl.semaphore_signal(barrier, inc=1, device_id=place, device_id_type=pl.DeviceIdType.MESH)
    pl.semaphore_wait(barrier, len(peers) + len(others))

    def exchange(group, offset):
        copies = []
        for place, slots, d in group:
            copy = pltpu.make_async_remote_copy(
                src_ref=slots.at[0],
                dst_ref=slots.at[d],
                send_sem=sems.at[offset + d],
                recv_sem=recv_sems.at[offset + d],
                device_id=place,
                device_id_type=pl.DeviceIdType.MESH,
            )
            copy.start()
            copies.append(copy)
        for copy in copies:
            copy.wait()

    col_slots[0] = value_ref[...]
    exchange(peers, 0)
    row_slots[0] = jnp.sum(col_slots[...], axis=0)
    exchange(others, cols)
    out_ref[...] = jnp.sum(row_slots[...], axis=0)


def sum_everywhere(value):
    rows, cols = lax.axis_size("row"), lax.axis_size("col")
    return pl.pallas_call(
        functools.partial(sum_kernel, (rows, cols)),
        out_shape=jax.ShapeDtypeStruct(value.shape, jnp.float32),
        in_specs=[pl.BlockSpec(memory_space=pltpu.VMEM)],
        out_specs=pl.BlockSpec(memory_space=pltpu.VMEM),
        scratch_shapes=[
            pltpu.VMEM((cols,) + value.shape, jnp.float32),
            pltpu.VMEM((rows,) + value.shape, jnp.float32),
            pltpu.SemaphoreType.DMA((rows + cols,)),
            pltpu.SemaphoreType.DMA((rows + cols,)),
        ],
        compiler_params=pltpu.CompilerParams(collective_id=0, has_side_effects=True),
        name="sum_everywhere",
    )(value)


def operator_matrix(tensor, narrow):
    width, sites = tensor.shape[0], tensor.shape[2]
    matrix = jnp.pad(
        jnp.transpose(tensor, (2, 0, 3, 1)),
        ((0, 0), (0, M_PAD - width), (0, 0), (0, narrow - width)),
    )
    return matrix.reshape(sites * M_PAD, sites * narrow)


def on_device(
    psi, env_left, env_right, first_site_operator, mpo_right, block_mask, left_live, right_live
):
    block_rows = env_left.shape[2]
    lanes = env_right.shape[4]
    mpo_width = env_left.shape[4]
    states = psi.shape[1]
    sites = first_site_operator.shape[2]
    inside = lax.iota(jnp.int32, block_rows)
    live = (
        (block_mask[0, 0] > 0)
        & (inside < left_live[0])[:, None]
        & (lax.iota(jnp.int32, lanes) < right_live[0])[None, :]
    )
    masked = psi * live[:, None, :].astype(jnp.bfloat16)
    low = from_behind(masked, "col", 1)
    high = from_behind(masked, "col", -1)
    env_next = shared_from_behind(env_left[0, 0], -1)
    env_prev = shared_from_behind(env_left[0, 2], 1)
    by_t = jnp.transpose(
        masked.reshape(block_rows, sites, sites, lanes), (2, 0, 1, 3)
    ).reshape(sites, block_rows, sites * lanes)
    psi_rows = jnp.concatenate(
        [by_t, from_behind(by_t, "row", -1), from_behind(by_t, "row", 1)], axis=1
    )
    widened = jnp.concatenate([low, masked, high], axis=2).reshape(
        block_rows * states, 3 * lanes
    )
    two = right_part(
        widened, jnp.transpose(env_right[0], (0, 2, 1, 3)), operator_matrix(mpo_right, N_PAD)
    )
    env_all = jnp.concatenate([env_left[0, 1], env_next, env_prev], axis=0)
    env_all = jnp.pad(env_all, ((0, 0), (0, 0), (0, M_PAD - mpo_width))).reshape(
        3 * block_rows, block_rows * M_PAD
    )
    first = operator_matrix(first_site_operator, M_PAD)
    totals, products = [], []
    for t in range(sites):
        own, sent, product = left_part(two, first, env_all, psi_rows, t)
        from_prev = from_behind(sent[:block_rows], "row", 1)
        from_next = from_behind(sent[block_rows:], "row", -1)
        totals.append((own, from_prev, from_next))
        products.append(product)
    numerator = jnp.sum(sum(products))
    masked_float = masked.astype(jnp.float32)
    denominator = jnp.sum(masked_float * masked_float)
    sums = jnp.where(lax.broadcasted_iota(jnp.int32, (8, 128), 0) < 4, numerator, denominator)
    sums = sum_everywhere(sums)
    quotient = sums[0, 0] / (sums[4, 0] + 1e-06)
    applied = jnp.stack(
        [
            (own + from_prev.astype(jnp.float32) + from_next.astype(jnp.float32)).reshape(
                block_rows, sites, lanes
            )
            for own, from_prev, from_next in totals
        ],
        axis=2,
    ).reshape(block_rows, states, lanes)
    applied = applied * live[:, None, :].astype(jnp.float32)
    return (
        applied.astype(jnp.bfloat16),
        (applied - quotient * masked_float).astype(jnp.bfloat16),
        quotient,
    )


def solution(mesh):
    return jax.shard_map(
        on_device,
        mesh=mesh,
        in_specs=(
            P("row", None, "col"),
            P("row", None, None, None, None),
            P("col", None, None, None, None),
            P(),
            P(),
            P("row", "col"),
            P("row"),
            P("col"),
        ),
        out_specs=(P("row", None, "col"), P("row", None, "col"), P()),
        check_vma=False,
    )
```

time: 983 us -> 200 us (0.20)
  waiting for transfers between devices: 733 us -> 27.3 us
  matrix products: 82.9 us -> 0 us
  Pallas kernels: 0 us -> 72.9 us
  local copies, waits for them, and re-layouts: 94.7 us -> 29 us
  blocking collectives: 46.6 us -> 0 us
  starting transfers between devices: 14.9 us -> 40.1 us
  between operations: 5.21 us -> 18.9 us
    ppermute x2 -> x14, waiting for transfers between devices: 732 us -> 27.3 us  [from_behind(): return lax.ppermute(block, axis, route)]
    dot_general x6 -> x0, matrix products: 82.9 us -> none  [the longest x3 27.7 us: couple_left(): jnp.dot(coupling.reshape(block_rows, block_rows * mpo_width), operand, pr...]
    pallas_call x0 -> x6, Pallas kernels: none -> 72.9 us  [the longest x4 35.4 us: left_part(): pl.pallas_call(left_kernel, grid=(steps,), in_specs=[pl.BlockSpec((1, CHU...]
    reshape x2 -> x5, local copies, waits for them, and re-layouts: 59 us -> 7.33 us  [the longest x1 6.63 us: on_device(): jnp.pad(env_all, ((0, 0), (0, 0), (0, M_PAD - mpo_width)))]
    psum x1 -> x0, blocking collectives: 46.6 us -> none  [on_device(): lax.psum((jnp.sum(psi_float * applied), jnp.sum(psi_float * psi_float)),...]
    ppermute x2 -> x14, starting transfers between devices: 11.2 us -> 40 us  [from_behind(): return lax.ppermute(block, axis, route)]
    convert_element_type x1 -> x0, local copies, waits for them, and re-layouts: 17.6 us -> none  [on_device(): third_section = jnp.einsum('dquo,woqzj->wduzj', first_site_operator, seco...]
  transfers between devices with their start and end apart: 4 -> 16, of which waited for: 2 -> 4; matrix products, arithmetic and copies ran while one was open for 3% -> 9% of each run, Pallas kernels for 0% -> 19%
where the time goes in v1:
time: 200 us; the launch traced here: 199 us
  Pallas kernels  72.9 us (36%)
  starting transfers between devices  40.1 us (20%)
  local copies, waits for them, and re-layouts  29 us (14%)
  waiting for transfers between devices  27.3 us (14%)
  between operations  18.9 us (9%)
  other arithmetic  10.6 us (5%)
    ppermute x14, starting transfers between devices, from_behind(): return lax.ppermute(block, axis, route)  40 us
    pallas_call x4, Pallas kernels, left_part(): pl.pallas_call(left_kernel, grid=(steps,), in_specs=[pl.BlockSpec((1, CHU...  35.4 us
    ppermute x14, waiting for transfers between devices, from_behind(): return lax.ppermute(block, axis, route)  27.3 us
    pallas_call x1, Pallas kernels, right_part(): pl.pallas_call(right_kernel, grid=(rows // block,), in_specs=[pl.BlockSpe...  24.5 us
    pallas_call x1, Pallas kernels, sum_everywhere(): pl.pallas_call(functools.partial(sum_kernel, (rows, cols)), out_shape=jax...  13 us
    unnamed x21, local copies, waits for them, and re-layouts  7.53 us
    reshape x1, local copies, waits for them, and re-layouts, on_device(): jnp.pad(env_all, ((0, 0), (0, 0), (0, M_PAD - mpo_width)))  6.63 us
    all_gather x2, local copies, waits for them, and re-layouts, shared_from_behind(): return lax.all_gather(moved, 'col', axis=0, tiled=True)  5.41 us
  transfers between devices with their start and end apart: 16, of which 4 were waited for; matrix products, arithmetic and copies ran while one was open for 9% of the time, Pallas kernels for 19%

profile of v1, /device:TPU:0, one launch (start us, length us, event | category | flops | bytes accessed | tf_op | source)
XLA Modules:
  0.0 198.8 jit_solution(18092246601239679917)
XLA Ops:
  7.2 3.3 %fusion.8 = (bf16[1,1,128,128,34]{3,2,4,1,0:T(8,128)(2,1)S(1)}, bf16[1,1,128,128,34]{3,2,4,1,0:T(8,128)(2,1)}, bf16[1,1,128,128,34]{3,2,4,1,0:T(8,128)(2,1)S(1)}) fusion(bf16[1,3,128,128,34]{3,2,4,1,0:T(8,128)(2,1)} %param.9), kind=kLoop, calls=%fused_computation.31 | loop fusion | bytes 6684672 | tf_op jit(solution)/shard_map/slice | solution.py:266
  11.8 10.2 %collective-permute-done.2 = bf16[32,128,34]{1,0,2:T(8,128)(2,1)S(1)} collective-permute-done((bf16[32,128,34]{1,0,2:T(8,128)(2,1)S(1)}, bf16[32,128,34]{1,0,2:T(8,128)(2,1)S(1)}, u32[]{:S(2)}, u32[]{:S(2)}) %collective-permute-start.2) | collective-permute-done | bytes 278560 | tf_op jit(solution)/shard_map/ppermute | solution.py:18
  28.1 6.0 %collective-permute-start.5 = (bf16[4,128,512]{2,1,0:T(8,128)(2,1)S(1)}, bf16[4,128,512]{2,1,0:T(8,128)(2,1)}, u32[]{:S(2)}, u32[]{:S(2)}) collective-permute-start(bf16[4,128,512]{2,1,0:T(8,128)(2,1)S(1)} %reshape.98), channel_id=1, source_target_pairs={{0,4},{4,8},{8,12},{12,16},{16,20},{20,24},{24,28},{1,5},{5,9},{9,... | collective-permute-start | bytes 1572872 | tf_op jit(solution)/shard_map/ppermute | solution.py:18
  35.0 4.8 %collective-permute-start.3 = (bf16[32,128,34]{1,0,2:T(8,128)(2,1)S(1)}, bf16[32,128,34]{1,0,2:T(8,128)(2,1)}, u32[]{:S(2)}, u32[]{:S(2)}) collective-permute-start(bf16[32,128,34]{1,0,2:T(8,128)(2,1)S(1)} %dynamic-slice_bitcast_fusion), channel_id=1, source_target_pairs={{0,4},{4,8},{8,12},{12,16},{16,20},{20,24},{24,28},{1,5},{5,9},{9,... | collective-permute-start | bytes 835592 | tf_op jit(solution)/shard_map/ppermute | solution.py:18
  41.1 3.9 %collective-permute-start = (bf16[128,16,128]{2,1,0:T(8,128)(2,1)S(1)}, bf16[128,16,128]{2,1,0:T(8,128)(2,1)}, u32[]{:S(2)}, u32[]{:S(2)}) collective-permute-start(bf16[128,16,128]{2,1,0:T(8,128)(2,1)S(1)} %get-tuple-element.28), channel_id=1, source_target_pairs={{0,1},{1,2},{2,3},{4,5},{5,6},{6,7},{8,9},{9,10},{10,11},{12,13},{... | collective-permute-start | bytes 1572872 | tf_op jit(solution)/shard_map/ppermute | solution.py:18
  46.5 2.0 %copy.42 = bf16[1,1,128,128,34]{2,4,3,1,0:T(8,128)(2,1)} copy(bf16[1,1,128,128,34]{3,2,4,1,0:T(8,128)(2,1)S(1)} %get-tuple-element.29) | data formatting | bytes 2228224
  48.5 11.2 %collective-permute-done.3 = bf16[32,128,34]{1,0,2:T(8,128)(2,1)} collective-permute-done((bf16[32,128,34]{1,0,2:T(8,128)(2,1)S(1)}, bf16[32,128,34]{1,0,2:T(8,128)(2,1)}, u32[]{:S(2)}, u32[]{:S(2)}) %collective-permute-start.3) | collective-permute-done | bytes 278560 | tf_op jit(solution)/shard_map/ppermute | solution.py:18
  63.6 24.5 %right_part.1.two_ref = bf16[4,24576,128]{2,1,0:T(8,128)(2,1)} custom-call(bf16[2048,384]{1,0:T(8,128)(2,1)S(1)} %bitcast.23, bf16[3,34,128,128]{3,2,1,0:T(8,128)(2,1)S(1)} %bitcast.24, bf16[192,160]{1,0:T(8,128)(2,1)S(1)} %reshape.100.site_ref), custom_call_target="tpu_custom_call" | custom-call | flops 13690208256 | bytes 25165824 | tf_op jit(solution)/shard_map/right_part/pallas_call | solution.py:77
  88.1 2.7 %copy.32 = bf16[128,128,34]{0,2,1:T(8,128)(2,1)} copy(bf16[128,128,34]{1,0,2:T(8,128)(2,1)} %all-gather.3.cloned.1.call-done) | data formatting | bytes 2228224 | tf_op jit(solution)/shard_map/all_gather | solution.py:25
  90.8 2.7 %copy.33 = bf16[128,128,34]{0,2,1:T(8,128)(2,1)} copy(bf16[128,128,34]{1,0,2:T(8,128)(2,1)} %all-gather.5.cloned.1.call-done) | data formatting | bytes 2228224 | tf_op jit(solution)/shard_map/all_gather | solution.py:25
  93.5 4.1 %fusion.4 = bf16[384,128,48]{0,2,1:T(8,128)(2,1)} fusion(bf16[128,128,34]{0,2,1:T(8,128)(2,1)} %copy.33, bf16[128,128,34]{0,2,1:T(8,128)(2,1)} %copy.32, bf16[128,128,34]{0,2,1:T(8,128)(2,1)} %bitcast.27), kind=kLoop, calls=%fused_computation.5 | loop fusion | flops 23592960 | bytes 8060928 | tf_op jit(solution)/shard_map/concatenate | solution.py:266
  97.6 6.6 %copy.35.env_ref = bf16[384,6144]{1,0:T(8,128)(2,1)} copy(bf16[384,6144]{0,1:T(8,128)(2,1)} %bitcast.25) | data formatting | bytes 9437184 | tf_op jit(solution)/shard_map/reshape | solution.py:267
  104.2 2.3 %copy-done = bf16[384,6144]{1,0:T(8,128)(2,1)S(1)} copy-done((bf16[384,6144]{1,0:T(8,128)(2,1)S(1)}, bf16[384,6144]{1,0:T(8,128)(2,1)}, u32[]{:S(2)}) %copy-start) | copy-done | bytes 4718616
  106.5 8.8 %left_part.7 = (f32[128,512]{1,0:T(8,128)S(1)}, bf16[256,512]{1,0:T(8,128)(2,1)S(1)}, f32[8,512]{1,0:T(8,128)S(1)}) custom-call(bf16[4,24576,128]{2,1,0:T(8,128)(2,1)} %right_part.1.two_ref, bf16[192,192]{1,0:T(8,128)(2,1)S(1)} %reshape.95.site_ref, bf16[384,6144]{1,0:T(8,128)(2,1)S(1)} %copy-done, ...), custom_call_target="tpu_custom_call" | custom-call | flops 4831838208 | bytes 11010048 | tf_op jit(solution)/shard_map/left_part/pallas_call | solution.py:142
  115.4 8.9 %left_part.6 = (f32[128,512]{1,0:T(8,128)S(1)}, bf16[256,512]{1,0:T(8,128)(2,1)S(1)}, f32[8,512]{1,0:T(8,128)S(1)}) custom-call(bf16[4,24576,128]{2,1,0:T(8,128)(2,1)} %right_part.1.two_ref, bf16[192,192]{1,0:T(8,128)(2,1)S(1)} %reshape.95.site_ref, bf16[384,6144]{1,0:T(8,128)(2,1)S(1)} %copy-done, ...), custom_call_target="tpu_custom_call" | custom-call | flops 4831838208 | bytes 11010048 | tf_op jit(solution)/shard_map/left_part/pallas_call | solution.py:142
  124.2 8.9 %left_part.5 = (f32[128,512]{1,0:T(8,128)S(1)}, bf16[256,512]{1,0:T(8,128)(2,1)S(1)}, f32[8,512]{1,0:T(8,128)S(1)}) custom-call(bf16[4,24576,128]{2,1,0:T(8,128)(2,1)} %right_part.1.two_ref, bf16[192,192]{1,0:T(8,128)(2,1)S(1)} %reshape.95.site_ref, bf16[384,6144]{1,0:T(8,128)(2,1)S(1)} %copy-done, ...), custom_call_target="tpu_custom_call" | custom-call | flops 4831838208 | bytes 11010048 | tf_op jit(solution)/shard_map/left_part/pallas_call | solution.py:142
  133.1 8.9 %left_part.4 = (f32[128,512]{1,0:T(8,128)S(1)}, bf16[256,512]{1,0:T(8,128)(2,1)S(1)}, f32[8,512]{1,0:T(8,128)S(1)}) custom-call(bf16[4,24576,128]{2,1,0:T(8,128)(2,1)} %right_part.1.two_ref, bf16[192,192]{1,0:T(8,128)(2,1)S(1)} %reshape.95.site_ref, bf16[384,6144]{1,0:T(8,128)(2,1)S(1)} %copy-done, ...), custom_call_target="tpu_custom_call" | custom-call | flops 4831838208 | bytes 11010048 | tf_op jit(solution)/shard_map/left_part/pallas_call | solution.py:142
  142.0 4.5 %collective-permute-start.12 = (bf16[128,512]{1,0:T(8,128)(2,1)S(1)}, bf16[128,512]{1,0:T(8,128)(2,1)S(1)}, u32[]{:S(2)}, u32[]{:S(2)}) collective-permute-start(bf16[128,512]{1,0:T(8,128)(2,1)S(1)} %get-tuple-element.40), channel_id=1, source_target_pairs={{0,4},{4,8},{8,12},{12,16},{16,20},{20,24},{24,28},{1,5},{5,9},{9,... | collective-permute-start | bytes 393224 | tf_op jit(solution)/shard_map/ppermute | solution.py:18
  147.8 4.6 %collective-permute-start.10 = (bf16[128,512]{1,0:T(8,128)(2,1)S(1)}, bf16[128,512]{1,0:T(8,128)(2,1)S(1)}, u32[]{:S(2)}, u32[]{:S(2)}) collective-permute-start(bf16[128,512]{1,0:T(8,128)(2,1)S(1)} %get-tuple-element.38), channel_id=1, source_target_pairs={{0,4},{4,8},{8,12},{12,16},{16,20},{20,24},{24,28},{1,5},{5,9},{9,... | collective-permute-start | bytes 393224 | tf_op jit(solution)/shard_map/ppermute | solution.py:18
  156.3 13.0 %sum_everywhere.1 = f32[8,128]{1,0:T(8,128)} custom-call(f32[8,128]{1,0:T(8,128)} %iota.19.value_ref), custom_call_target="tpu_custom_call" | custom-call | tf_op jit(solution)/shard_map/sum_everywhere/pallas_call | solution.py:210
  170.6 2.7 %collective-permute-start.8 = (bf16[128,512]{1,0:T(8,128)(2,1)S(1)}, bf16[128,512]{1,0:T(8,128)(2,1)S(1)}, u32[]{:S(2)}, u32[]{:S(2)}) collective-permute-start(bf16[128,512]{1,0:T(8,128)(2,1)S(1)} %get-tuple-element.36), channel_id=1, source_target_pairs={{0,4},{4,8},{8,12},{12,16},{16,20},{20,24},{24,28},{1,5},{5,9},{9,... | collective-permute-start | bytes 393224 | tf_op jit(solution)/shard_map/ppermute | solution.py:18
  176.0 4.6 %collective-permute-start.6 = (bf16[128,512]{1,0:T(8,128)(2,1)S(1)}, bf16[128,512]{1,0:T(8,128)(2,1)S(1)}, u32[]{:S(2)}, u32[]{:S(2)}) collective-permute-start(bf16[128,512]{1,0:T(8,128)(2,1)S(1)} %get-tuple-element.34), channel_id=1, source_target_pairs={{0,4},{4,8},{8,12},{12,16},{16,20},{20,24},{24,28},{1,5},{5,9},{9,... | collective-permute-start | bytes 393224 | tf_op jit(solution)/shard_map/ppermute | solution.py:18
  182.3 1.9 collective-permute-done.6
  184.2 4.0 %collective-permute-done.7 = bf16[128,512]{1,0:T(8,128)(2,1)S(1)} collective-permute-done((bf16[128,512]{1,0:T(8,128)(2,1)S(1)}, bf16[128,512]{1,0:T(8,128)(2,1)S(1)}, u32[]{:S(2)}, u32[]{:S(2)}) %collective-permute-start.7) | collective-permute-done | bytes 131104 | tf_op jit(solution)/shard_map/ppermute | solution.py:18
  (74 shorter events, 25.0 us)
Async XLA Ops:
  7.2 80.9 %all-gather.3.cloned.1.call-start = ((), (), s32[]{:S(2)}) async-start(), calls=%async_computation | async-start | bytes 1392640 | tf_op jit(solution)/shard_map/all_gather | solution.py:25
  7.2 18.3 %copy-start.4 = (bf16[128,16,128]{2,1,0:T(8,128)(2,1)S(1)}, bf16[128,16,128]{2,1,0:T(8,128)(2,1)}, u32[]{:S(2)}) copy-start(bf16[128,16,128]{2,1,0:T(8,128)(2,1)} %param.8) | copy-start | bytes 1572868
  10.5 11.5 %collective-permute-start.2 = (bf16[32,128,34]{1,0,2:T(8,128)(2,1)S(1)}, bf16[32,128,34]{1,0,2:T(8,128)(2,1)S(1)}, u32[]{:S(2)}, u32[]{:S(2)}) collective-permute-start(bf16[32,128,34]{1,0,2:T(8,128)(2,1)S(1)} %dynamic-slice_bitcast_fusion.1), channel_id=1, source_target_pairs={{4,0},{8,4},{12,8},{16,12},{20,16},{24,20},{28,24},{5,1},{9,5},{13... | collective-permute-start | bytes 835592 | tf_op jit(solution)/shard_map/ppermute | solution.py:18
  22.0 0.7 copy-start.5
  22.8 68.0 %all-gather.5.cloned.1.call-start = ((), (), s32[]{:S(2)}) async-start(), calls=%async_computation.1 | async-start | bytes 1392640 | tf_op jit(solution)/shard_map/all_gather | solution.py:25
  26.4 35.8 %copy-start.2 = (bf16[128,16,128]{2,1,0:T(8,128)(2,1)}, bf16[128,16,128]{2,1,0:T(8,128)(2,1)S(1)}, u32[]{:S(2)}) copy-start(bf16[128,16,128]{2,1,0:T(8,128)(2,1)S(1)} %get-tuple-element.28) | copy-start | bytes 1572868
  26.4 18.6 %copy-start.7 = (bf16[34,34,4,4]{1,3,2,0:T(4,128)(2,1)S(1)}, bf16[34,34,4,4]{1,3,2,0:T(4,128)(2,1)}, u32[]{:S(2)}) copy-start(bf16[34,34,4,4]{1,3,2,0:T(4,128)(2,1)} %param.11) | copy-start | bytes 110980
  26.8 33.0 %collective-permute-start.4 = (bf16[4,128,512]{2,1,0:T(8,128)(2,1)S(1)}, bf16[4,128,512]{2,1,0:T(8,128)(2,1)}, u32[]{:S(2)}, u32[]{:S(2)}) collective-permute-start(bf16[4,128,512]{2,1,0:T(8,128)(2,1)S(1)} %reshape.98), channel_id=1, source_target_pairs={{4,0},{8,4},{12,8},{16,12},{20,16},{24,20},{28,24},{5,1},{9,5},{13... | collective-permute-start | bytes 1572872 | tf_op jit(solution)/shard_map/ppermute | solution.py:18
  28.1 32.8 %collective-permute-start.5 = (bf16[4,128,512]{2,1,0:T(8,128)(2,1)S(1)}, bf16[4,128,512]{2,1,0:T(8,128)(2,1)}, u32[]{:S(2)}, u32[]{:S(2)}) collective-permute-start(bf16[4,128,512]{2,1,0:T(8,128)(2,1)S(1)} %reshape.98), channel_id=1, source_target_pairs={{0,4},{4,8},{8,12},{12,16},{16,20},{20,24},{24,28},{1,5},{5,9},{9,... | collective-permute-start | bytes 1572872 | tf_op jit(solution)/shard_map/ppermute | solution.py:18
  35.0 24.7 %collective-permute-start.3 = (bf16[32,128,34]{1,0,2:T(8,128)(2,1)S(1)}, bf16[32,128,34]{1,0,2:T(8,128)(2,1)}, u32[]{:S(2)}, u32[]{:S(2)}) collective-permute-start(bf16[32,128,34]{1,0,2:T(8,128)(2,1)S(1)} %dynamic-slice_bitcast_fusion), channel_id=1, source_target_pairs={{0,4},{4,8},{8,12},{12,16},{16,20},{20,24},{24,28},{1,5},{5,9},{9,... | collective-permute-start | bytes 835592 | tf_op jit(solution)/shard_map/ppermute | solution.py:18
  39.8 22.3 %collective-permute-start.1 = (bf16[128,16,128]{2,1,0:T(8,128)(2,1)S(1)}, bf16[128,16,128]{2,1,0:T(8,128)(2,1)}, u32[]{:S(2)}, u32[]{:S(2)}) collective-permute-start(bf16[128,16,128]{2,1,0:T(8,128)(2,1)S(1)} %get-tuple-element.28), channel_id=1, source_target_pairs={{1,0},{2,1},{3,2},{5,4},{6,5},{7,6},{9,8},{10,9},{11,10},{13,12},{... | collective-permute-start | bytes 1572872 | tf_op jit(solution)/shard_map/ppermute | solution.py:18
  41.1 21.0 %collective-permute-start = (bf16[128,16,128]{2,1,0:T(8,128)(2,1)S(1)}, bf16[128,16,128]{2,1,0:T(8,128)(2,1)}, u32[]{:S(2)}, u32[]{:S(2)}) collective-permute-start(bf16[128,16,128]{2,1,0:T(8,128)(2,1)S(1)} %get-tuple-element.28), channel_id=1, source_target_pairs={{0,1},{1,2},{2,3},{4,5},{5,6},{6,7},{8,9},{9,10},{10,11},{12,13},{... | collective-permute-start | bytes 1572872 | tf_op jit(solution)/shard_map/ppermute | solution.py:18
  60.9 2.7 %copy-start.1 = (bf16[1,3,128,34,128]{4,2,3,1,0:T(8,128)(2,1)S(1)}, bf16[1,3,128,34,128]{4,2,3,1,0:T(8,128)(2,1)}, u32[]{:S(2)}) copy-start(bf16[1,3,128,34,128]{4,2,3,1,0:T(8,128)(2,1)} %param.10) | copy-start | bytes 10027012
  104.2 2.3 %copy-start = (bf16[384,6144]{1,0:T(8,128)(2,1)S(1)}, bf16[384,6144]{1,0:T(8,128)(2,1)}, u32[]{:S(2)}) copy-start(bf16[384,6144]{1,0:T(8,128)(2,1)} %copy.35.env_ref) | copy-start | bytes 14155780
  142.0 32.6 %collective-permute-start.12 = (bf16[128,512]{1,0:T(8,128)(2,1)S(1)}, bf16[128,512]{1,0:T(8,128)(2,1)S(1)}, u32[]{:S(2)}, u32[]{:S(2)}) collective-permute-start(bf16[128,512]{1,0:T(8,128)(2,1)S(1)} %get-tuple-element.40), channel_id=1, source_target_pairs={{0,4},{4,8},{8,12},{12,16},{16,20},{20,24},{24,28},{1,5},{5,9},{9,... | collective-permute-start | bytes 393224 | tf_op jit(solution)/shard_map/ppermute | solution.py:18
  146.5 29.4 %collective-permute-start.13 = (bf16[128,512]{1,0:T(8,128)(2,1)S(1)}, bf16[128,512]{1,0:T(8,128)(2,1)S(1)}, u32[]{:S(2)}, u32[]{:S(2)}) collective-permute-start(bf16[128,512]{1,0:T(8,128)(2,1)S(1)} %get-tuple-element.41), channel_id=1, source_target_pairs={{4,0},{8,4},{12,8},{16,12},{20,16},{24,20},{28,24},{5,1},{9,5},{13... | collective-permute-start | bytes 393224 | tf_op jit(solution)/shard_map/ppermute | solution.py:18
  147.8 32.8 %collective-permute-start.10 = (bf16[128,512]{1,0:T(8,128)(2,1)S(1)}, bf16[128,512]{1,0:T(8,128)(2,1)S(1)}, u32[]{:S(2)}, u32[]{:S(2)}) collective-permute-start(bf16[128,512]{1,0:T(8,128)(2,1)S(1)} %get-tuple-element.38), channel_id=1, source_target_pairs={{0,4},{4,8},{8,12},{12,16},{16,20},{20,24},{24,28},{1,5},{5,9},{9,... | collective-permute-start | bytes 393224 | tf_op jit(solution)/shard_map/ppermute | solution.py:18
  152.4 29.6 %collective-permute-start.11 = (bf16[128,512]{1,0:T(8,128)(2,1)S(1)}, bf16[128,512]{1,0:T(8,128)(2,1)S(1)}, u32[]{:S(2)}, u32[]{:S(2)}) collective-permute-start(bf16[128,512]{1,0:T(8,128)(2,1)S(1)} %get-tuple-element.39), channel_id=1, source_target_pairs={{4,0},{8,4},{12,8},{16,12},{20,16},{24,20},{28,24},{5,1},{9,5},{13... | collective-permute-start | bytes 393224 | tf_op jit(solution)/shard_map/ppermute | solution.py:18
  170.6 11.6 %collective-permute-start.8 = (bf16[128,512]{1,0:T(8,128)(2,1)S(1)}, bf16[128,512]{1,0:T(8,128)(2,1)S(1)}, u32[]{:S(2)}, u32[]{:S(2)}) collective-permute-start(bf16[128,512]{1,0:T(8,128)(2,1)S(1)} %get-tuple-element.36), channel_id=1, source_target_pairs={{0,4},{4,8},{8,12},{12,16},{16,20},{20,24},{24,28},{1,5},{5,9},{9,... | collective-permute-start | bytes 393224 | tf_op jit(solution)/shard_map/ppermute | solution.py:18
  174.6 7.5 %collective-permute-start.9 = (bf16[128,512]{1,0:T(8,128)(2,1)S(1)}, bf16[128,512]{1,0:T(8,128)(2,1)S(1)}, u32[]{:S(2)}, u32[]{:S(2)}) collective-permute-start(bf16[128,512]{1,0:T(8,128)(2,1)S(1)} %get-tuple-element.37), channel_id=1, source_target_pairs={{4,0},{8,4},{12,8},{16,12},{20,16},{24,20},{28,24},{5,1},{9,5},{13... | collective-permute-start | bytes 393224 | tf_op jit(solution)/shard_map/ppermute | solution.py:18
  176.0 8.2 %collective-permute-start.6 = (bf16[128,512]{1,0:T(8,128)(2,1)S(1)}, bf16[128,512]{1,0:T(8,128)(2,1)S(1)}, u32[]{:S(2)}, u32[]{:S(2)}) collective-permute-start(bf16[128,512]{1,0:T(8,128)(2,1)S(1)} %get-tuple-element.34), channel_id=1, source_target_pairs={{0,4},{4,8},{8,12},{12,16},{16,20},{20,24},{24,28},{1,5},{5,9},{9,... | collective-permute-start | bytes 393224 | tf_op jit(solution)/shard_map/ppermute | solution.py:18
  180.7 7.5 %collective-permute-start.7 = (bf16[128,512]{1,0:T(8,128)(2,1)S(1)}, bf16[128,512]{1,0:T(8,128)(2,1)S(1)}, u32[]{:S(2)}, u32[]{:S(2)}) collective-permute-start(bf16[128,512]{1,0:T(8,128)(2,1)S(1)} %get-tuple-element.35), channel_id=1, source_target_pairs={{4,0},{8,4},{12,8},{16,12},{20,16},{24,20},{28,24},{5,1},{9,5},{13... | collective-permute-start | bytes 393224 | tf_op jit(solution)/shard_map/ppermute | solution.py:18
  188.6 1.0 copy-start.3
  188.6 1.0 copy-start.6
Sparse Core Ops, SparseCore 0:
  22.9 18.4 all-gather.2
  59.9 18.4 all-gather.4

commit v2 on v1

v2 whole, which is shorter than its diff:
```python
import functools

import jax
import jax.numpy as jnp
from jax import lax
from jax.experimental import pallas as pl
from jax.experimental.pallas import tpu as pltpu
from jax.sharding import PartitionSpec as P

CHUNK = 16
N_PAD = 40
M_PAD = 48


def from_behind(block, axis, distance):
    devices = range(lax.axis_size(axis))
    route = [(i - distance, i) for i in devices if i - distance in devices]
    return lax.ppermute(block, axis, route)


def right_kernel(psi_ref, env_ref, site_ref, two_ref, one):
    rows = psi_ref.shape[0]
    depth, width, inside, lanes = env_ref.shape
    sites = site_ref.shape[1] // N_PAD

    @pl.when(pl.program_id(0) == 0)
    def _():
        one[...] = jnp.zeros_like(one)

    for w in range(0, width, 2):
        env = jnp.concatenate(
            [
                jnp.concatenate([env_ref[k, w + j] for k in range(depth)], axis=0)
                for j in range(2)
            ],
            axis=1,
        )
        found = jnp.dot(psi_ref[...], env, preferred_element_type=jnp.float32)
        for j in range(2):
            one[pl.ds(w + j, rows, stride=N_PAD), :] = found[:, j * lanes : (j + 1) * lanes]

    tall = sites * N_PAD

    def pair(i, _):
        start = pl.multiple_of(i * (2 * tall), 2 * tall)
        operand = jnp.concatenate(
            [one[pl.ds(start + j * tall, tall), :].astype(jnp.bfloat16) for j in range(2)], axis=1
        )
        found = jnp.dot(
            site_ref[...], operand, preferred_element_type=jnp.float32
        ).astype(jnp.bfloat16)
        for t in range(sites):
            for j in range(2):
                spot = pl.multiple_of((i * 2 + j) * M_PAD, M_PAD)
                two_ref[t, pl.ds(spot, M_PAD), :] = found[
                    t * M_PAD : (t + 1) * M_PAD, j * lanes : (j + 1) * lanes
                ]
        return 0

    lax.fori_loop(0, rows // sites // 2, pair, 0, unroll=8)


def right_part(widened, env, site):
    rows, depth = widened.shape
    lanes = env.shape[3]
    sites = site.shape[0] // M_PAD
    states = sites * sites
    block = CHUNK * states
    tall = rows // sites * M_PAD
    return pl.pallas_call(
        right_kernel,
        grid=(rows // block,),
        in_specs=[
            pl.BlockSpec((block, depth), lambda i: (i, 0)),
            pl.BlockSpec(env.shape, lambda i: (0, 0, 0, 0)),
            pl.BlockSpec(site.shape, lambda i: (0, 0)),
        ],
        out_specs=pl.BlockSpec((sites, CHUNK * sites * M_PAD, lanes), lambda i: (0, i, 0)),
        out_shape=jax.ShapeDtypeStruct((sites, tall, lanes), jnp.bfloat16),
        scratch_shapes=[pltpu.VMEM((block * N_PAD, lanes), jnp.float32)],
        compiler_params=pltpu.CompilerParams(vmem_limit_bytes=48 * 2**20),
        cost_estimate=pl.CostEstimate(
            flops=2 * rows * depth * env.shape[1] * lanes * 2,
            bytes_accessed=2 * sites * tall * lanes,
            transcendentals=0,
        ),
        name="right_part",
    )(widened, env, site)


def left_kernel(
    two_ref, site_ref, own_env_ref, far_env_ref, psi_ref,
    own_ref, next_ref, prev_ref, dot_ref, three, total,
):
    step = pl.program_id(1)
    lanes = two_ref.shape[2]
    sites = site_ref.shape[0] // M_PAD
    tall = sites * M_PAD
    block_rows = own_ref.shape[1]
    share = block_rows // lax.axis_size("col")

    for x in range(0, CHUNK, 2):
        operand = jnp.concatenate(
            [two_ref[0, (x + j) * tall : (x + j + 1) * tall, :] for j in range(2)], axis=1
        )
        found = jnp.dot(
            site_ref[...], operand, preferred_element_type=jnp.float32
        ).astype(jnp.bfloat16)
        for j in range(2):
            for r in range(sites):
                three[(x + j) * M_PAD : (x + j + 1) * M_PAD, r * lanes : (r + 1) * lanes] = found[
                    r * M_PAD : (r + 1) * M_PAD, j * lanes : (j + 1) * lanes
                ]
    env = jnp.concatenate([own_env_ref[...], far_env_ref[...]], axis=0)
    part = jnp.dot(env, three[...], preferred_element_type=jnp.float32)

    @pl.when(step == 0)
    def _():
        total[...] = part

    @pl.when(step > 0)
    def _():
        total[...] += part

    @pl.when(step == pl.num_programs(1) - 1)
    def _():
        def far(direction):
            starts = range(block_rows + direction * share, 3 * block_rows, 2 * share)
            return jnp.concatenate([total[at : at + share, :] for at in starts], axis=0)

        def psi_of(place):
            return psi_ref[0, place * block_rows : (place + 1) * block_rows, :].astype(jnp.float32)

        def folded(value):
            return jnp.sum(value.reshape(-1, 8, value.shape[1]), axis=0)

        own = total[:block_rows, :]
        to_next, to_prev = far(0), far(1)
        own_psi = psi_of(0)
        own_ref[0] = own
        next_ref[0] = to_next.astype(jnp.bfloat16)
        prev_ref[0] = to_prev.astype(jnp.bfloat16)
        dot_ref[0, :8, :] = folded(own_psi * own + psi_of(1) * to_next + psi_of(2) * to_prev)
        dot_ref[0, 8:, :] = folded(own_psi * own_psi)


def left_part(two, site, own_env, far_env, psi_rows, base, count):
    lanes = two.shape[2]
    sites = site.shape[0] // M_PAD
    steps = two.shape[1] // (CHUNK * sites * M_PAD)
    block_rows, wide = own_env.shape[0], sites * lanes
    result = pl.BlockSpec((1, block_rows, wide), lambda t, i: (t, 0, 0))
    return pl.pallas_call(
        left_kernel,
        grid=(count, steps),
        in_specs=[
            pl.BlockSpec((1, CHUNK * sites * M_PAD, lanes), lambda t, i: (base + t, i, 0)),
            pl.BlockSpec(site.shape, lambda t, i: (0, 0)),
            pl.BlockSpec((block_rows, CHUNK * M_PAD), lambda t, i: (0, i)),
            pl.BlockSpec((2 * block_rows, CHUNK * M_PAD), lambda t, i: (0, i)),
            pl.BlockSpec((1, 3 * block_rows, wide), lambda t, i: (base + t, 0, 0)),
        ],
        out_specs=[
            result,
            result,
            result,
            pl.BlockSpec((1, 16, wide), lambda t, i: (t, 0, 0)),
        ],
        out_shape=[
            jax.ShapeDtypeStruct((count, block_rows, wide), jnp.float32),
            jax.ShapeDtypeStruct((count, block_rows, wide), jnp.bfloat16),
            jax.ShapeDtypeStruct((count, block_rows, wide), jnp.bfloat16),
            jax.ShapeDtypeStruct((count, 16, wide), jnp.float32),
        ],
        scratch_shapes=[
            pltpu.VMEM((CHUNK * M_PAD, wide), jnp.bfloat16),
            pltpu.VMEM((3 * block_rows, wide), jnp.float32),
        ],
        compiler_params=pltpu.CompilerParams(vmem_limit_bytes=40 * 2**20),
        cost_estimate=pl.CostEstimate(
            flops=2 * count * 3 * block_rows * own_env.shape[1] * wide * 2,
            bytes_accessed=count * (2 * two.shape[1] * lanes + 6 * own_env.size),
            transcendentals=0,
        ),
        name="left_part",
    )(two, site, own_env, far_env, psi_rows)


def neighbours(axis):
    at, count = lax.axis_index(axis), lax.axis_size(axis)
    return at, at > 0, at < count - 1


def place_at(axis, distance):
    row, col = lax.axis_index("row"), lax.axis_index("col")
    return (row + distance, col) if axis == "row" else (row, col + distance)


def remote(source, target, send_sem, recv_sem, place):
    return pltpu.make_async_remote_copy(
        src_ref=source,
        dst_ref=target,
        send_sem=send_sem,
        recv_sem=recv_sem,
        device_id=place,
        device_id_type=pl.DeviceIdType.MESH,
    )


def shift_both(axis, up_ref, down_ref, slots, send_sems, recv_sems):
    _, has_prev, has_next = neighbours(axis)
    up = remote(up_ref, slots.at[0], send_sems.at[0], recv_sems.at[0], place_at(axis, 1))
    down = remote(down_ref, slots.at[1], send_sems.at[1], recv_sems.at[1], place_at(axis, -1))

    def start():
        pl.when(has_next)(up.start)
        pl.when(has_prev)(down.start)

    def finish():
        @pl.when(has_next)
        def _():
            up.wait_send()
            down.wait_recv()

        @pl.when(has_prev)
        def _():
            down.wait_send()
            up.wait_recv()

        @pl.when(jnp.logical_not(has_prev))
        def _():
            slots[0] = jnp.zeros_like(slots[0])

        @pl.when(jnp.logical_not(has_next))
        def _():
            slots[1] = jnp.zeros_like(slots[1])

    return start, finish


def first_kernel(psi_ref, env_ref, psi_out, env_out, psi_slots, env_slots, sends, receives):
    barrier = pltpu.get_barrier_semaphore()
    expected = 0
    for axis in ("row", "col"):
        _, has_prev, has_next = neighbours(axis)
        for there, distance in ((has_prev, -1), (has_next, 1)):
            place = place_at(axis, distance)

            @pl.when(there)
            def _():
                pl.semaphore_signal(
                    barrier, inc=1, device_id=place, device_id_type=pl.DeviceIdType.MESH
                )

            expected = expected + there.astype(jnp.int32)
    pl.semaphore_wait(barrier, expected)
    start_psi, finish_psi = shift_both(
        "col", psi_ref, psi_ref, psi_slots, sends.at[0], receives.at[0]
    )
    start_env, finish_env = shift_both(
        "row", env_ref.at[1], env_ref.at[0], env_slots, sends.at[1], receives.at[1]
    )
    start_env()
    start_psi()
    finish_psi()
    psi_out[...] = psi_slots[...]
    finish_env()
    env_out[...] = env_slots[...]


def vmem_call(kernel, out_shape, scratch_shapes, collective_id, name):
    spec = pl.BlockSpec(memory_space=pltpu.VMEM)
    return pl.pallas_call(
        kernel,
        out_shape=out_shape,
        in_specs=[spec] * (2 if collective_id == 1 else 3),
        out_specs=[spec] * len(out_shape),
        scratch_shapes=scratch_shapes,
        compiler_params=pltpu.CompilerParams(
            collective_id=collective_id, has_side_effects=True, vmem_limit_bytes=32 * 2**20
        ),
        name=name,
    )


def first_moves(psi, env):
    shapes = [(2,) + psi.shape, env.shape]
    return vmem_call(
        first_kernel,
        [jax.ShapeDtypeStruct(shape, jnp.bfloat16) for shape in shapes],
        [pltpu.VMEM(shape, jnp.bfloat16) for shape in shapes]
        + [pltpu.SemaphoreType.DMA((2, 2))] * 2,
        1,
        "first_moves",
    )(psi, env)


def last_kernel(
    sizes, next_ref, prev_ref, dot_ref, sums_out, quotient_out,
    slots, col_slots, row_slots, far_sends, far_receives, sends, receives,
):
    rows, cols = sizes
    row, col = lax.axis_index("row"), lax.axis_index("col")
    lanes = col_slots.shape[2]
    peers = [((row, lax.rem(col + d, cols)), d) for d in range(1, cols)]
    others = [((lax.rem(row + d, rows), col), d) for d in range(1, rows)]
    barrier = pltpu.get_barrier_semaphore()
    for place, _ in peers + others:
        pl.semaphore_signal(barrier, inc=1, device_id=place, device_id_type=pl.DeviceIdType.MESH)
    pl.semaphore_wait(barrier, len(peers) + len(others))

    def exchange(group, buffer, at, offset):
        copies = [
            remote(
                buffer.at[at], buffer.at[at], sends.at[offset + d], receives.at[offset + d], place
            )
            for place, d in group
        ]
        for copy in copies:
            copy.start()
        return copies

    dots = jnp.sum(dot_ref[...], axis=0)
    col_slots[col] = sum(dots[:, at : at + lanes] for at in range(0, dots.shape[1], lanes))
    copies = exchange(peers, col_slots, col, 0)
    start, finish = shift_both("row", next_ref, prev_ref, slots, far_sends, far_receives)
    start()
    for copy in copies:
        copy.wait()
    row_slots[row] = jnp.sum(col_slots[...], axis=0)
    for copy in exchange(others, row_slots, row, cols):
        copy.wait()
    whole = jnp.sum(row_slots[...], axis=0)
    quotient = jnp.sum(whole[:8], keepdims=True) / (jnp.sum(whole[8:], keepdims=True) + 1e-6)
    quotient_out[...] = jnp.broadcast_to(quotient, quotient_out.shape)
    finish()
    sums_out[...] = slots[0].astype(jnp.float32) + slots[1].astype(jnp.float32)


def last_moves(to_next, to_prev, dots, lanes):
    rows, cols = lax.axis_size("row"), lax.axis_size("col")
    return vmem_call(
        functools.partial(last_kernel, (rows, cols)),
        [
            jax.ShapeDtypeStruct(to_next.shape, jnp.float32),
            jax.ShapeDtypeStruct((8, lanes), jnp.float32),
        ],
        [
            pltpu.VMEM((2,) + to_next.shape, jnp.bfloat16),
            pltpu.VMEM((cols, 16, lanes), jnp.float32),
            pltpu.VMEM((rows, 16, lanes), jnp.float32),
            pltpu.SemaphoreType.DMA((2,)),
            pltpu.SemaphoreType.DMA((2,)),
            pltpu.SemaphoreType.DMA((rows + cols,)),
            pltpu.SemaphoreType.DMA((rows + cols,)),
        ],
        2,
        "last_moves",
    )(to_next, to_prev, dots)


def operator_matrix(tensor, narrow):
    width, sites = tensor.shape[0], tensor.shape[2]
    matrix = jnp.pad(
        jnp.transpose(tensor, (2, 0, 3, 1)),
        ((0, 0), (0, M_PAD - width), (0, 0), (0, narrow - width)),
    )
    return matrix.reshape(sites * M_PAD, sites * narrow)


def padded_couplings(coupling):
    lead, width = coupling.shape[:-1], coupling.shape[-1]
    wide = jnp.pad(coupling, [(0, 0)] * len(lead) + [(0, M_PAD - width)])
    return wide.reshape(lead[:-1] + (lead[-1] * M_PAD,))


def on_device(
    psi, env_left, env_right, first_site_operator, mpo_right, block_mask, left_live, right_live
):
    block_rows = env_left.shape[2]
    lanes = env_right.shape[4]
    states = psi.shape[1]
    sites = first_site_operator.shape[2]
    inside = lax.iota(jnp.int32, block_rows)
    live = (
        (block_mask[0, 0] > 0)
        & (inside < left_live[0])[:, None]
        & (lax.iota(jnp.int32, lanes) < right_live[0])[None, :]
    )
    masked = psi * live[:, None, :].astype(jnp.bfloat16)
    flat = masked.reshape(block_rows * states, lanes)
    share = block_rows // lax.axis_size("col")
    shares = lax.dynamic_slice_in_dim(
        env_left[0], lax.axis_index("col") * share, share, 1
    )
    wings = padded_couplings(jnp.stack([shares[0], shares[2]]))
    sides, moved = first_moves(flat, wings)
    moved = moved[::-1].reshape(2 * share, block_rows * M_PAD)
    far_env = lax.all_gather(moved, "col", axis=0, tiled=True)
    own_env = padded_couplings(env_left[0, 1])
    by_t = jnp.transpose(
        masked.reshape(block_rows, sites, sites, lanes), (2, 0, 1, 3)
    ).reshape(sites, block_rows, sites * lanes)
    by_t, sides = lax.optimization_barrier((by_t, sides))
    psi_rows = jnp.concatenate(
        [by_t, from_behind(by_t, "row", -1), from_behind(by_t, "row", 1)], axis=1
    )
    widened = jnp.concatenate([sides[0], flat, sides[1]], axis=1)
    two = right_part(
        widened, jnp.transpose(env_right[0], (0, 2, 1, 3)), operator_matrix(mpo_right, N_PAD)
    )
    first = operator_matrix(first_site_operator, M_PAD)
    half = sites // 2
    own_a, next_a, prev_a, dots_a = left_part(two, first, own_env, far_env, psi_rows, 0, half)
    from_prev = from_behind(next_a, "row", 1)
    from_next = from_behind(prev_a, "row", -1)
    own_b, next_b, prev_b, dots_b = left_part(two, first, own_env, far_env, psi_rows, half, half)
    far_b, ratio = last_moves(next_b, prev_b, jnp.concatenate([dots_a, dots_b]), lanes)
    quotient = ratio[0, 0]
    far_a = from_prev.astype(jnp.float32) + from_next.astype(jnp.float32)
    applied = jnp.concatenate([own_a + far_a, own_b + far_b])
    applied = jnp.transpose(
        applied.reshape(sites, block_rows, sites, lanes), (1, 2, 0, 3)
    ).reshape(block_rows, states, lanes)
    applied = applied * live[:, None, :].astype(jnp.float32)
    return (
        applied.astype(jnp.bfloat16),
        (applied - quotient * masked.astype(jnp.float32)).astype(jnp.bfloat16),
        quotient,
    )


def solution(mesh):
    return jax.shard_map(
        on_device,
        mesh=mesh,
        in_specs=(
            P("row", None, "col"),
            P("row", None, None, None, None),
            P("col", None, None, None, None),
            P(),
            P(),
            P("row", "col"),
            P("row"),
            P("col"),
        ),
        out_specs=(P("row", None, "col"), P("row", None, "col"), P()),
        check_vma=False,
    )
```

time: 200 us -> 154 us (0.77)
  starting transfers between devices: 40.1 us -> 12.4 us
  waiting for transfers between devices: 27.3 us -> 0.05 us
  Pallas kernels: 72.9 us -> 96.5 us
  other arithmetic: 10.6 us -> 2.58 us
  local copies, waits for them, and re-layouts: 29 us -> 24.5 us
  between operations: 18.9 us -> 16.3 us
    ppermute x14 -> x4, starting transfers between devices: 40 us -> 12.4 us  [from_behind(): return lax.ppermute(block, axis, route)]
    ppermute x14 -> x4, waiting for transfers between devices: 27.3 us -> 0.01 us  [from_behind(): return lax.ppermute(block, axis, route)]
    pallas_call x5 -> x4, Pallas kernels: 48.4 us -> 72 us  [the longest x2 34 us: left_part(): pl.pallas_call(left_kernel, grid=(count, steps), in_specs=[pl.BlockSpec((...]
    all_gather x2 -> x0, local copies, waits for them, and re-layouts: 5.41 us -> none  [shared_from_behind(): return lax.all_gather(moved, 'col', axis=0, tiled=True)]
    concatenate x2 -> x3, other arithmetic: 5.48 us -> 0.29 us  [the longest x1 0.21 us: on_device(): widened = jnp.concatenate([sides[0], flat, sides[1]], axis=1)]
    pad x0 -> x2, local copies, waits for them, and re-layouts: none -> 2.08 us  [padded_couplings(): wide = jnp.pad(coupling, [(0, 0)] * len(lead) + [(0, M_PAD - width)])]
    unnamed x21 -> x20, local copies, waits for them, and re-layouts: 7.53 us -> 9.48 us
    slice x6 -> x4, local copies, waits for them, and re-layouts: 4.62 us -> 2.85 us  [the longest x2 1.25 us: on_device(): own_env = padded_couplings(env_left[0, 1])]
  transfers between devices with their start and end apart: 16 -> 5, of which waited for: 4 -> 0; matrix products, arithmetic and copies ran while one was open for 9% -> 5% of each run, Pallas kernels for 19% -> 39%
where the time goes in v2:
time: 154 us; the launch traced here: 152 us
  Pallas kernels  96.5 us (63%)
  local copies, waits for them, and re-layouts  24.5 us (16%)
  between operations  16.3 us (11%)
  starting transfers between devices  12.4 us (8%)
  other arithmetic  2.58 us (2%)
    pallas_call x2, Pallas kernels, left_part(): pl.pallas_call(left_kernel, grid=(count, steps), in_specs=[pl.BlockSpec((...  34 us
    pallas_call x1, Pallas kernels, right_part(): pl.pallas_call(right_kernel, grid=(rows // block,), in_specs=[pl.BlockSpe...  24.5 us
    pallas_call x1, Pallas kernels, first_moves(): vmem_call(first_kernel, [jax.ShapeDtypeStruct(shape, jnp.bfloat16) for sh...  20.5 us
    pallas_call x1, Pallas kernels, last_moves(): vmem_call(functools.partial(last_kernel, (rows, cols)), [jax.ShapeDtypeSt...  17.5 us
    ppermute x4, starting transfers between devices, from_behind(): return lax.ppermute(block, axis, route)  12.4 us
    unnamed x20, local copies, waits for them, and re-layouts  9.48 us
    reshape x2, local copies, waits for them, and re-layouts, padded_couplings(): return wide.reshape(lead[:-1] + (lead[-1] * M_PAD,))  5.27 us
  transfers between devices with their start and end apart: 5, of which 0 were waited for; matrix products, arithmetic and copies ran while one was open for 5% of the time, Pallas kernels for 39%

profile of v2, /device:TPU:0, one launch (start us, length us, event | category | flops | bytes accessed | tf_op | source)
XLA Modules:
  0.0 152.3 jit_solution(10339288945524137070)
XLA Ops:
  7.2 1.1 dynamic-slice_bitcast_fusion.1
  8.4 1.2 copy.29
  9.6 1.9 %pad.16.clone = bf16[2,32,128,48]{3,2,1,0:T(8,128)(2,1)} pad(bf16[2,32,128,34]{3,2,1,0:T(8,128)(2,1)S(1)} %copy.29, bf16[]{:T(256)} %constant.14.clone.1), padding=0_0x0_0x0_0x0_14 | pad | bytes 1343490 | tf_op jit(solution)/shard_map/jit(_pad)/pad | solution.py:373
  11.5 4.6 %reshape.103.env_ref = bf16[2,32,6144]{2,1,0:T(8,128)(2,1)S(1)} reshape(bf16[2,32,128,48]{3,2,1,0:T(8,128)(2,1)} %pad.16.clone) | data formatting | bytes 1572864 | tf_op jit(solution)/shard_map/reshape | solution.py:374
  18.2 20.5 %first_moves.1 = (bf16[2,2048,128]{2,1,0:T(8,128)(2,1)S(1)}, bf16[2,32,6144]{2,1,0:T(8,128)(2,1)S(1)}) custom-call(bf16[2048,128]{1,0:T(8,128)(2,1)S(1)} %bitcast.31, bf16[2,32,6144]{2,1,0:T(8,128)(2,1)S(1)} %reshape.103.env_ref), custom_call_target="tpu_custom_call" | custom-call | tf_op jit(solution)/shard_map/first_moves/pallas_call | solution.py:288
  38.8 1.0 rev.3
  39.9 1.0 reshape.101
  40.9 1.3 collective-permute-start
  42.2 5.8 %collective-permute-start.1 = (bf16[4,128,512]{2,1,0:T(8,128)(2,1)}, bf16[4,128,512]{2,1,0:T(8,128)(2,1)}, u32[]{:S(2)}, u32[]{:S(2)}) collective-permute-start(bf16[4,128,512]{2,1,0:T(8,128)(2,1)} %reshape.101), channel_id=1, source_target_pairs={{0,4},{4,8},{8,12},{12,16},{16,20},{20,24},{24,28},{1,5},{5,9},{9,... | collective-permute-start | bytes 1572872 | tf_op jit(solution)/shard_map/ppermute | solution.py:18
  48.7 2.2 %copy-done = bf16[1,3,128,34,128]{4,2,3,1,0:T(8,128)(2,1)S(1)} copy-done((bf16[1,3,128,34,128]{4,2,3,1,0:T(8,128)(2,1)S(1)}, bf16[1,3,128,34,128]{4,2,3,1,0:T(8,128)(2,1)}, u32[]{:S(2)}) %copy-start) | copy-done | bytes 3342360
  50.8 24.5 %right_part.1.two_ref = bf16[4,24576,128]{2,1,0:T(8,128)(2,1)} custom-call(bf16[2048,384]{1,0:T(8,128)(2,1)S(1)} %pad_maximum_fusion.psi_ref, bf16[3,34,128,128]{3,2,1,0:T(8,128)(2,1)S(1)} %bitcast.34, bf16[192,160]{1,0:T(8,128)(2,1)S(1)} %reshape.110.site_ref), custom_call_target="tpu_custom_call" | custom-call | flops 13690208256 | bytes 25165824 | tf_op jit(solution)/shard_map/right_part/pallas_call | solution.py:70
  75.4 1.2 slice-done
  76.6 1.4 copy.28
  78.2 0.7 copy.23.own_env_ref
  79.4 1.1 constant_dynamic-update-slice_fusion.2
  80.5 1.1 constant_dynamic-update-slice_fusion.1
  81.6 1.1 constant_dynamic-update-slice_fusion.psi_ref
  82.7 1.9 %copy-done.1 = bf16[256,6144]{1,0:T(8,128)(2,1)S(1)} copy-done((bf16[256,6144]{1,0:T(8,128)(2,1)S(1)}, bf16[256,6144]{1,0:T(8,128)(2,1)}, u32[]{:S(2)}) %copy-start.1) | copy-done | bytes 3145752
  84.6 17.1 %left_part.2 = (f32[2,128,512]{2,1,0:T(8,128)S(1)}, bf16[2,128,512]{2,1,0:T(8,128)(2,1)S(1)}, bf16[2,128,512]{2,1,0:T(8,128)(2,1)S(1)}, f32[2,16,512]{2,1,0:T(8,128)S(1)}) custom-call(bf16[4,24576,128]{2,1,0:T(8,128)(2,1)} %right_part.1.two_ref, bf16[192,192]{1,0:T(8,128)(2,1)S(1)} %reshape.105.site_ref, bf16[128,6144]{1,0:T(8,128)(2,1)S(1)} %copy.23.own_env_ref, ...), custom_call_target="tpu_custom_call" | custom-call | flops 9663676416 | bytes 22020096 | tf_op jit(solution)/shard_map/left_part/pallas_call | solution.py:153
  101.7 4.0 %collective-permute-start.2 = (bf16[2,128,512]{2,1,0:T(8,128)(2,1)S(1)}, bf16[2,128,512]{2,1,0:T(8,128)(2,1)S(1)}, u32[]{:S(2)}, u32[]{:S(2)}) collective-permute-start(bf16[2,128,512]{2,1,0:T(8,128)(2,1)S(1)} %get-tuple-element.22), channel_id=1, source_target_pairs={{0,4},{4,8},{8,12},{12,16},{16,20},{20,24},{24,28},{1,5},{5,9},{9,... | collective-permute-start | bytes 786440 | tf_op jit(solution)/shard_map/ppermute | solution.py:18
  105.6 1.3 collective-permute-start.3
  106.9 16.9 %left_part.3 = (f32[2,128,512]{2,1,0:T(8,128)S(1)}, bf16[2,128,512]{2,1,0:T(8,128)(2,1)S(1)}, bf16[2,128,512]{2,1,0:T(8,128)(2,1)S(1)}, f32[2,16,512]{2,1,0:T(8,128)S(1)}) custom-call(bf16[4,24576,128]{2,1,0:T(8,128)(2,1)} %right_part.1.two_ref, bf16[192,192]{1,0:T(8,128)(2,1)S(1)} %reshape.105.site_ref, bf16[128,6144]{1,0:T(8,128)(2,1)S(1)} %copy.23.own_env_ref, ...), custom_call_target="tpu_custom_call" | custom-call | flops 9663676416 | bytes 22020096 | tf_op jit(solution)/shard_map/left_part/pallas_call | solution.py:153
  123.9 17.5 %last_moves.1 = (f32[2,128,512]{2,1,0:T(8,128)S(1)}, f32[8,128]{1,0:T(8,128)S(1)}) custom-call(bf16[2,128,512]{2,1,0:T(8,128)(2,1)S(1)} %get-tuple-element.25.next_ref, bf16[2,128,512]{2,1,0:T(8,128)(2,1)S(1)} %get-tuple-element.26.prev_ref, f32[4,16,512]{2,1,0:T(8,128)S(1)} %pad_maximum_fusion.3.dot_ref), custom_call_target="tpu_custom_call" | custom-call | tf_op jit(solution)/shard_map/last_moves/pallas_call | solution.py:342
  143.6 1.9 %subtract_convert_fusion = (bf16[128,16,128]{2,1,0:T(8,128)(2,1)}, bf16[128,16,128]{2,1,0:T(8,128)(2,1)}) fusion(f32[128,16,128]{2,1,0:T(8,128)S(1)} %bitcast.37, f32[]{:T(128)} %bitcast.19, f32[128,128]{1,0:T(8,128)S(1)} %get-tuple-element.37, bf16[128,16,128]{2,1,0:T(8,128)(2,1)S(1)} %copy-done.4, bf16[128,128]{1,0:T(8,128)(2,1)S(1)} %get-tuple-element.38), kind=kLoop, calls=%fused_computation.2 | loop fusion | flops 1835008 | bytes 2719748 | tf_op jit(solution)/shard_map/convert_element_type | solution.py:428
  (41 shorter events, 3.9 us)
Async XLA Ops:
  7.2 75.5 %all-gather.2.cloned.1.call-start = ((), (), s32[]{:S(2)}) async-start(), calls=%async_computation | async-start | bytes 3932160 | tf_op jit(solution)/shard_map/all_gather | solution.py:399
  11.5 6.6 %copy-start.3 = (bf16[128,16,128]{2,1,0:T(8,128)(2,1)S(1)}, bf16[128,16,128]{2,1,0:T(8,128)(2,1)}, u32[]{:S(2)}) copy-start(bf16[128,16,128]{2,1,0:T(8,128)(2,1)} %param.8) | copy-start | bytes 1572868
  39.7 8.3 %copy-start.5 = (bf16[34,34,4,4]{1,3,2,0:T(4,128)(2,1)S(1)}, bf16[34,34,4,4]{1,3,2,0:T(4,128)(2,1)}, u32[]{:S(2)}) copy-start(bf16[34,34,4,4]{1,3,2,0:T(4,128)(2,1)} %param.12) | copy-start | bytes 110980
  40.9 39.5 %collective-permute-start = (bf16[4,128,512]{2,1,0:T(8,128)(2,1)}, bf16[4,128,512]{2,1,0:T(8,128)(2,1)}, u32[]{:S(2)}, u32[]{:S(2)}) collective-permute-start(bf16[4,128,512]{2,1,0:T(8,128)(2,1)} %reshape.101), channel_id=1, source_target_pairs={{4,0},{8,4},{12,8},{16,12},{20,16},{24,20},{28,24},{5,1},{9,5},{13... | collective-permute-start | bytes 1572872 | tf_op jit(solution)/shard_map/ppermute | solution.py:18
  42.2 39.3 %collective-permute-start.1 = (bf16[4,128,512]{2,1,0:T(8,128)(2,1)}, bf16[4,128,512]{2,1,0:T(8,128)(2,1)}, u32[]{:S(2)}, u32[]{:S(2)}) collective-permute-start(bf16[4,128,512]{2,1,0:T(8,128)(2,1)} %reshape.101), channel_id=1, source_target_pairs={{0,4},{4,8},{8,12},{12,16},{16,20},{20,24},{24,28},{1,5},{5,9},{9,... | collective-permute-start | bytes 1572872 | tf_op jit(solution)/shard_map/ppermute | solution.py:18
  48.3 2.5 %copy-start = (bf16[1,3,128,34,128]{4,2,3,1,0:T(8,128)(2,1)S(1)}, bf16[1,3,128,34,128]{4,2,3,1,0:T(8,128)(2,1)}, u32[]{:S(2)}) copy-start(bf16[1,3,128,34,128]{4,2,3,1,0:T(8,128)(2,1)} %param.10) | copy-start | bytes 10027012
  75.3 1.2 slice-start
  78.2 0.9 copy-start.6
  82.7 1.9 %copy-start.1 = (bf16[256,6144]{1,0:T(8,128)(2,1)S(1)}, bf16[256,6144]{1,0:T(8,128)(2,1)}, u32[]{:S(2)}) copy-start(bf16[256,6144]{1,0:T(8,128)(2,1)} %all-gather.2.cloned.1.call-done.far_env_ref) | copy-start | bytes 9437188
  84.6 22.4 %copy-start.2 = (bf16[256,6144]{1,0:T(8,128)(2,1)S(1)}, bf16[256,6144]{1,0:T(8,128)(2,1)}, u32[]{:S(2)}) copy-start(bf16[256,6144]{1,0:T(8,128)(2,1)} %all-gather.2.cloned.1.call-done.far_env_ref) | copy-start | bytes 9437188
  101.7 40.3 %collective-permute-start.2 = (bf16[2,128,512]{2,1,0:T(8,128)(2,1)S(1)}, bf16[2,128,512]{2,1,0:T(8,128)(2,1)S(1)}, u32[]{:S(2)}, u32[]{:S(2)}) collective-permute-start(bf16[2,128,512]{2,1,0:T(8,128)(2,1)S(1)} %get-tuple-element.22), channel_id=1, source_target_pairs={{0,4},{4,8},{8,12},{12,16},{16,20},{20,24},{24,28},{1,5},{5,9},{9,... | collective-permute-start | bytes 786440 | tf_op jit(solution)/shard_map/ppermute | solution.py:18
  105.6 36.3 %collective-permute-start.3 = (bf16[2,128,512]{2,1,0:T(8,128)(2,1)S(1)}, bf16[2,128,512]{2,1,0:T(8,128)(2,1)S(1)}, u32[]{:S(2)}, u32[]{:S(2)}) collective-permute-start(bf16[2,128,512]{2,1,0:T(8,128)(2,1)S(1)} %get-tuple-element.23), channel_id=1, source_target_pairs={{4,0},{8,4},{12,8},{16,12},{20,16},{24,20},{28,24},{5,1},{9,5},{13... | collective-permute-start | bytes 786440 | tf_op jit(solution)/shard_map/ppermute | solution.py:18
  142.5 1.0 copy-start.4
Sparse Core Ops, SparseCore 0:
  39.9 29.6 all-gather.1
